TPU v7x, 32 devices: a whole 2x2x4 slice. The times are simulated.
32 devices in a mesh: groups: 2 (over x), heads: 16 (over z, y, core).
Axes of the slice: x: 2, y: 2, z: 4, core: 2. Of those that a mesh axis runs over, the one named last changes fastest.
Arguments:
- hidden: bfloat16 [384, 6144], P('groups'), parts along dimension 0, may hold values from -6 to 6
- in_gain: float32 [1, 6144], replicated, may hold values from 0.1 to 1.9
- w_in: bfloat16 [1, 6144, 32768], P(None, 'heads'), may hold values from -0.078125 to 0.078125
- attn_gain: float32 [1, 8192], P(None, 'heads'), may hold values from 0.1 to 1.9
- w_out: bfloat16 [1, 8192, 6144], P(None, None, 'heads'), may hold values from -0.0625 to 0.0625
- slope_index: int32 [1, 64], P(None, 'heads'), may hold values from 8 to 29
Outputs:
- result: bfloat16 [384, 6144], P('groups'), parts along dimension 0
There are 2 independent parts, one for each index of `groups`. A program takes and returns all parts, laid end to end along the dimension named above; an argument that names none is the same for every part. Nothing has to cross between parts.
All inputs are finite; a program needn't handle non-finite values.
Results may differ from a plain program's by a relative error of at most 0.0038.
Values may be sent and summed in bfloat16 or wider, within the bound.
A program may use at most 192 MiB of HBM per device.

v0:
```python
import jax
import jax.numpy as jnp
from jax import lax
from jax.sharding import PartitionSpec as P

D = 6144


def on_device(hidden, in_gain, w_in, attn_gain, w_out, slope_index):
    members = lax.axis_size("heads")
    position = lax.axis_index("heads")
    shard_rows = w_in.shape[1]
    columns = attn_gain.shape[1]
    heads_local = slope_index.shape[1]
    head_width = columns // heads_local
    attn_width = columns * members
    stream = hidden
    owned_in = lax.all_to_all(
        w_in[0].reshape(shard_rows, 4, members, columns),
        "heads",
        split_axis=2,
        concat_axis=0,
        tiled=True,
    )
    owned_in = owned_in.reshape(D, 4 * columns)
    widened = stream.astype(jnp.float32)
    tokens_all = widened.shape[0]
    scale = lax.rsqrt(jnp.mean(widened * widened, axis=1, keepdims=True) + 1e-06)
    normed = (widened * scale * in_gain[0][None, :]).astype(jnp.bfloat16)
    proj = jnp.dot(normed, owned_in, preferred_element_type=jnp.float32)
    query = (
        jax.nn.silu(proj[:, :columns])
        .astype(jnp.bfloat16)
        .reshape(tokens_all, heads_local, head_width)
    )
    keys = (
        jax.nn.silu(proj[:, columns : 2 * columns])
        .astype(jnp.bfloat16)
        .reshape(tokens_all, heads_local, head_width)
    )
    values = (
        jax.nn.silu(proj[:, 2 * columns : 3 * columns])
        .astype(jnp.bfloat16)
        .reshape(tokens_all, heads_local, head_width)
    )
    gate = proj[:, 3 * columns :]
    slopes = jnp.exp2(-0.5 * slope_index[0].astype(jnp.float32))
    positions = jnp.arange(tokens_all, dtype=jnp.int32)
    offset = (positions[:, None] - positions[None, :]).astype(jnp.float32)
    decay = jnp.where(
        offset[None] >= 0.0, jnp.exp(-slopes[:, None, None] * jnp.maximum(offset, 0.0)[None]), 0.0
    )
    scores = jnp.einsum("thd,shd->hts", query, keys, preferred_element_type=jnp.float32)
    weights = (scores * decay).astype(jnp.bfloat16)
    attn = jnp.einsum("hts,shd->thd", weights, values, preferred_element_type=jnp.float32).reshape(
        tokens_all, columns
    )
    total = lax.psum(jnp.sum(attn * attn, axis=1), "heads")
    mixed = (
        attn
        * lax.rsqrt(total[:, None] / attn_width + 1e-06)
        * attn_gain[0][None, :]
        * jax.nn.sigmoid(gate)
    ).astype(jnp.bfloat16)
    owned_out = lax.all_to_all(
        w_out[0].reshape(members, columns, w_out.shape[2]),
        "heads",
        split_axis=0,
        concat_axis=2,
        tiled=True,
    )
    owned_out = owned_out.reshape(columns, D)
    share_rows = tokens_all // members

    def term(begin, amount, weights_out=owned_out, source=mixed):
        return jnp.dot(source, weights_out, preferred_element_type=jnp.float32)

    share = lax.psum_scatter(
        term(jnp.int32(0), lax.axis_size("heads") * share_rows),
        "heads",
        scatter_dimension=0,
        tiled=True,
    )
    own_rows = lax.dynamic_slice_in_dim(widened, position * share_rows, share_rows, 0)
    updated = (own_rows + share).astype(jnp.bfloat16)
    stream = lax.all_gather(updated, "heads", axis=0, tiled=True)
    return stream


def solution(mesh):
    placed = (
        P("groups", None),
        P(),
        P(None, "heads", None),
        P(None, "heads"),
        P(None, None, "heads"),
        P(None, "heads"),
    )
    return jax.shard_map(
        on_device, mesh=mesh, in_specs=placed, out_specs=P("groups", None), check_vma=False
    )
```

profile of v0, /device:TPU:0, one launch (start us, length us, event | category | flops | bytes accessed | tf_op | source)
XLA Modules:
  0.0 954.4 jit_solution(10360959247559715601)
XLA Ops:
  6.5 7.4 all-to-all-start.1
  14.0 32.5 %copy.24 = bf16[1,384,32768]{1,2,0:T(8,128)(2,1)} copy(bf16[1,384,32768]{2,1,0:T(8,128)(2,1)} %param.8) | data formatting | bytes 50331648 | tf_op args[2]
  46.5 20.9 %copy.25 = bf16[384,4,16,512]{0,3,1,2:T(8,128)(2,1)} copy(bf16[384,4,16,512]{0,3,2,1:T(8,128)(2,1)} %bitcast.66) | data formatting | bytes 50331648 | tf_op jit(solution)/shard_map/reshape;squeeze | solution.py:19
  67.4 0.0 copy-start.4
  67.4 0.0 copy-start
  67.4 60.8 %all-to-all-done.1 = bf16[16,512,384]{2,1,0:T(8,128)(2,1)} async-done(((bf16[16,512,384]{2,1,0:T(8,128)(2,1)}), bf16[16,512,384]{2,1,0:T(8,128)(2,1)}, u32[]{:S(2)}, u32[]{:S(2)}) %all-to-all-start.1) | async-done | bytes 6291488 | tf_op jit(solution)/shard_map/all_to_all | solution.py:65
  128.2 28.1 %all-to-all-start = ((bf16[384,4,16,512]{0,3,1,2:T(8,128)(2,1)}), bf16[384,4,16,512]{0,3,1,2:T(8,128)(2,1)}, u32[]{:S(2)}, u32[]{:S(2)}) async-start(bf16[384,4,16,512]{0,3,1,2:T(8,128)(2,1)} %copy.25), calls=%async_computation | async-start | bytes 50331648 | tf_op jit(solution)/shard_map/all_to_all | solution.py:18
  156.3 0.0 all-gather.3.cloned.1.call-start
  156.3 0.7 convert_compare_fusion
  157.0 0.0 copy-done.4
  157.1 0.0 copy-done
  157.1 0.6 multiply_reduce_fusion
  157.6 8.6 copy.31
  166.3 432.8 %all-to-all-done = bf16[384,4,16,512]{0,3,1,2:T(8,128)(2,1)} async-done(((bf16[384,4,16,512]{0,3,1,2:T(8,128)(2,1)}), bf16[384,4,16,512]{0,3,1,2:T(8,128)(2,1)}, u32[]{:S(2)}, u32[]{:S(2)}) %all-to-all-start) | async-done | bytes 25165856 | tf_op jit(solution)/shard_map/all_to_all | solution.py:18
  599.1 21.3 %copy.26 = bf16[16,384,4,1,512]{1,0,4,2,3:T(8,128)(2,1)S(1)} copy(bf16[16,384,4,1,512]{1,4,2,0,3:T(8,128)(2,1)} %bitcast.3) | data formatting | bytes 50331648 | tf_op jit(solution)/shard_map/all_to_all | solution.py:18
  620.5 0.0 copy-start.3
  620.5 10.6 %copy.36 = bf16[256,8,16,384]{3,1,2,0:T(8,128)(2,1)} copy(bf16[256,8,16,384]{3,2,1,0:T(8,128)(2,1)S(1)} %bitcast.65) | data formatting | bytes 50331648
  631.1 0.0 copy-done.3
  631.1 0.0 copy-start.1
  631.1 14.4 %fusion.1 = f32[192,2048]{1,0:T(8,128)} fusion(bf16[6144,2048]{0,1:T(8,128)(2,1)} %bitcast.67, f32[6144]{0:T(1024)S(1)} %bitcast.71, f32[192]{0:T(256)S(1)} %add_rsqrt_fusion.1, bf16[192,6144]{1,0:T(8,128)(2,1)S(1)} %copy-done), kind=kOutput, calls=%fused_computation.2 | convolution fusion | flops 4836556800 | bytes 29123328 | tf_op jit(solution)/shard_map/dot_general | solution.py:30
  645.5 1.5 fusion.39
  647.0 1.3 fusion.17
  648.3 131.9 %psum.7 = f32[192]{0:T(256)S(1)} all-reduce(f32[192]{0:T(256)S(1)} %get-tuple-element.8), channel_id=1, replica_groups=mesh['groups'=2,'heads'=16] {'heads'}, use_global_device_ids=true, to_apply=%region_2.3 | all-reduce | flops 192 | bytes 1536 | tf_op jit(solution)/shard_map/psum | solution.py:58
  780.3 0.0 copy-done.1
  780.3 7.3 fusion.23
  787.6 65.5 %fusion = f32[16,6144]{1,0:T(8,128)S(1)} fusion(f32[192,6144]{1,0:T(8,128)} %fusion.23), kind=kCustom, calls=%all-reduce-scatter | all-reduce-scatter fusion | flops 1572865 | bytes 5112320
  853.0 0.0 copy-start.2
  853.1 6.2 collective-permute-start
  859.3 5.0 collective-permute-start.1
  864.3 2.0 collective-permute-start.2
  866.3 2.1 collective-permute-start.3
  868.4 2.7 convert_element_type.44
  871.1 0.0 copy-done.2
  871.1 0.6 dynamic-slice.4
  872.3 4.9 collective-permute-done.3
  877.2 0.0 collective-permute-done
  877.2 0.0 collective-permute-done.1
  877.2 1.7 collective-permute-done.2
  878.9 8.0 concatenate
  886.9 1.8 fusion.22
  888.7 0.0 all-gather.3.cloned.1.call-update
  888.8 54.6 %all-gather.3.cloned.1.call-done = bf16[16,12,6144]{2,1,0:T(8,128)(2,1)} async-done(((bf16[1,12,6144]{2,1,0:T(8,128)(2,1)}), bf16[16,12,6144]{2,1,0:T(8,128)(2,1)}) %all-gather.3.cloned.1.call-update) | async-done | bytes 2359312 | tf_op jit(solution)/shard_map/all_gather | solution.py:86
  943.3 4.2 reshape.78
  (5 shorter events, 0.1 us)
Async XLA Ops:
  6.5 121.6 %all-to-all-start.1 = ((bf16[16,512,384]{2,1,0:T(8,128)(2,1)}), bf16[16,512,384]{2,1,0:T(8,128)(2,1)}, u32[]{:S(2)}, u32[]{:S(2)}) async-start(bf16[16,512,384]{2,1,0:T(8,128)(2,1)} %bitcast.69), calls=%async_computation.1 | async-start | bytes 12582912 | tf_op jit(solution)/shard_map/all_to_all | solution.py:65
  67.4 89.6 %copy-start.4 = (s32[1,4]{1,0:T(1,128)S(1)}, s32[1,4]{1,0:T(1,128)}, u32[]{:S(2)}) copy-start(s32[1,4]{1,0:T(1,128)} %param.11) | copy-start | bytes 52
  67.4 89.6 %copy-start = (bf16[192,6144]{1,0:T(8,128)(2,1)S(1)}, bf16[192,6144]{1,0:T(8,128)(2,1)}, u32[]{:S(2)}) copy-start(bf16[192,6144]{1,0:T(8,128)(2,1)} %param.6) | copy-start | bytes 7077892
  128.2 470.9 %all-to-all-start = ((bf16[384,4,16,512]{0,3,1,2:T(8,128)(2,1)}), bf16[384,4,16,512]{0,3,1,2:T(8,128)(2,1)}, u32[]{:S(2)}, u32[]{:S(2)}) async-start(bf16[384,4,16,512]{0,3,1,2:T(8,128)(2,1)} %copy.25), calls=%async_computation | async-start | bytes 50331648 | tf_op jit(solution)/shard_map/all_to_all | solution.py:18
  156.3 787.1 %all-gather.3.cloned.1.call-start = ((), (), s32[]{:S(2)}) async-start(), calls=%async_computation.2 | async-start | bytes 3342336 | tf_op jit(solution)/shard_map/all_gather | solution.py:86
  620.5 10.6 %copy-start.3 = (f32[1,6144]{1,0:T(1,128)S(1)}, f32[1,6144]{1,0:T(1,128)}, u32[]{:S(2)}) copy-start(f32[1,6144]{1,0:T(1,128)} %param.7) | copy-start | bytes 73732
  631.1 149.2 %copy-start.1 = (f32[1,512]{1,0:T(1,128)S(1)}, f32[1,512]{1,0:T(1,128)}, u32[]{:S(2)}) copy-start(f32[1,512]{1,0:T(1,128)} %param.9) | copy-start | bytes 6148
  853.0 18.0 %copy-start.2 = (u32[32]{0:T(128)S(1)}, u32[32]{0:T(128)}, u32[]{:S(2)}) copy-start(u32[32]{0:T(128)} %constant.35) | copy-start | bytes 388
  853.1 24.1 %collective-permute-start = (f32[16,6144]{1,0:T(8,128)S(1)}, f32[16,6144]{1,0:T(8,128)S(1)}, u32[]{:S(2)}, u32[]{:S(2)}) collective-permute-start(f32[16,6144]{1,0:T(8,128)S(1)} %fusion), channel_id=1, source_target_pairs={{0,1},{1,2},{2,3},{3,4},{4,5},{5,6},{6,7},{7,8},{8,9},{9,10},{10,1... | collective-permute-start | bytes 1179656
  859.3 17.9 %collective-permute-start.1 = (f32[16,6144]{1,0:T(8,128)S(1)}, f32[16,6144]{1,0:T(8,128)}, u32[]{:S(2)}, u32[]{:S(2)}) collective-permute-start(f32[16,6144]{1,0:T(8,128)S(1)} %fusion), channel_id=1, source_target_pairs={{0,2},{1,3},{2,4},{3,5},{4,6},{5,7},{6,8},{7,9},{8,10},{9,11},{10,... | collective-permute-start | bytes 1179656
  864.3 14.6 %collective-permute-start.2 = (f32[16,6144]{1,0:T(8,128)S(1)}, f32[16,6144]{1,0:T(8,128)}, u32[]{:S(2)}, u32[]{:S(2)}) collective-permute-start(f32[16,6144]{1,0:T(8,128)S(1)} %fusion), channel_id=1, source_target_pairs={{0,3},{1,4},{2,5},{3,6},{4,7},{5,8},{6,9},{7,10},{8,11},{9,12},{10... | collective-permute-start | bytes 1179656
  866.3 10.9 %collective-permute-start.3 = (f32[12,6144]{1,0:T(8,128)S(1)}, f32[12,6144]{1,0:T(8,128)}, u32[]{:S(2)}, u32[]{:S(2)}) collective-permute-start(f32[12,6144]{1,0:T(8,128)S(1)} %slice.20), channel_id=1, source_target_pairs={{0,4},{1,5},{2,6},{3,7},{4,8},{5,9},{6,10},{7,11},{8,12},{9,13},{1... | collective-permute-start | bytes 884744
Sparse Core Ops, SparseCore 0:
  888.9 54.4 all-gather.2
where the time goes:
time: 957 us; the launch traced here: 954 us
  waiting for transfers between devices  555 us (58%)
  blocking collectives  197 us (21%)
  local copies, waits for them, and re-layouts  107 us (11%)
  starting transfers between devices  50.9 us (5%)
  matrix products  23 us (2%)
  between operations  14.2 us (1%)
    all_to_all x1, waiting for transfers between devices, on_device(): lax.all_to_all(w_in[0].reshape(shard_rows, 4, members, columns), 'heads',...  433 us
    psum x1, blocking collectives, on_device(): total = lax.psum(jnp.sum(attn * attn, axis=1), 'heads')  132 us
    unnamed x1, blocking collectives  65.5 us
    all_to_all x1, waiting for transfers between devices, on_device(): lax.all_to_all(w_out[0].reshape(members, columns, w_out.shape[2]), 'heads...  60.8 us
    unnamed x16, local copies, waits for them, and re-layouts  56 us
    all_gather x1, waiting for transfers between devices, on_device(): stream = lax.all_gather(updated, 'heads', axis=0, tiled=True)  54.6 us
    all_to_all x1, starting transfers between devices, on_device(): lax.all_to_all(w_in[0].reshape(shard_rows, 4, members, columns), 'heads',...  28.1 us
    all_to_all x1, local copies, waits for them, and re-layouts, on_device(): lax.all_to_all(w_in[0].reshape(shard_rows, 4, members, columns), 'heads',...  21.3 us
  transfers between devices with their start and end apart: 7, of which 5 were waited for; matrix products, arithmetic and copies ran while one was open for 7% of the time, Pallas kernels for 0%

commit v1 on v0

v1 whole, which is shorter than its diff:
```python
import jax
import jax.numpy as jnp
from jax import lax
from jax.sharding import PartitionSpec as P

D = 6144


def on_device(hidden, in_gain, w_in, attn_gain, w_out, slope_index):
    members = lax.axis_size("heads")
    position = lax.axis_index("heads")
    shard_rows = w_in.shape[1]
    columns = attn_gain.shape[1]
    heads_local = slope_index.shape[1]
    head_width = columns // heads_local
    attn_width = columns * members
    out_columns = w_out.shape[2]
    widened = hidden.astype(jnp.float32)
    tokens = widened.shape[0]

    scale = lax.rsqrt(jnp.mean(widened * widened, axis=1, keepdims=True) + 1e-06)
    own_hidden = lax.dynamic_slice_in_dim(hidden, position * shard_rows, shard_rows, 1)
    own_gain = lax.dynamic_slice_in_dim(in_gain, position * shard_rows, shard_rows, 1)
    normed = (own_hidden.astype(jnp.float32) * scale * own_gain).astype(jnp.bfloat16)

    partial = jnp.dot(normed, w_in[0], preferred_element_type=jnp.float32).astype(jnp.bfloat16)
    partial = partial.reshape(tokens, 4, members, columns).transpose(2, 0, 1, 3)
    proj = lax.psum_scatter(partial, "heads", scatter_dimension=0, tiled=False)
    proj = proj.astype(jnp.float32)

    query = jax.nn.silu(proj[:, 0]).astype(jnp.bfloat16).reshape(tokens, heads_local, head_width)
    keys = jax.nn.silu(proj[:, 1]).astype(jnp.bfloat16).reshape(tokens, heads_local, head_width)
    values = jax.nn.silu(proj[:, 2]).astype(jnp.bfloat16).reshape(tokens, heads_local, head_width)
    gate = proj[:, 3]
    slopes = jnp.exp2(-0.5 * slope_index[0].astype(jnp.float32))
    positions = jnp.arange(tokens, dtype=jnp.int32)
    offset = (positions[:, None] - positions[None, :]).astype(jnp.float32)
    decay = jnp.where(
        offset[None] >= 0.0, jnp.exp(-slopes[:, None, None] * jnp.maximum(offset, 0.0)[None]), 0.0
    )
    scores = jnp.einsum("thd,shd->hts", query, keys, preferred_element_type=jnp.float32)
    weights = (scores * decay).astype(jnp.bfloat16)
    attn = jnp.einsum("hts,shd->thd", weights, values, preferred_element_type=jnp.float32).reshape(
        tokens, columns
    )
    total = lax.psum(jnp.sum(attn * attn, axis=1), "heads")
    mixed = (
        attn
        * lax.rsqrt(total[:, None] / attn_width + 1e-06)
        * attn_gain[0][None, :]
        * jax.nn.sigmoid(gate)
    ).astype(jnp.bfloat16)

    mixed_all = lax.all_gather(mixed, "heads", axis=0, tiled=False)
    w_blocks = w_out[0].reshape(members, columns, out_columns)
    update = jnp.einsum("mtc,mcd->td", mixed_all, w_blocks, preferred_element_type=jnp.float32)
    own = lax.dynamic_slice_in_dim(hidden, position * out_columns, out_columns, 1)
    updated = (own.astype(jnp.float32) + update).astype(jnp.bfloat16)
    return lax.all_gather(updated, "heads", axis=1, tiled=True)


def solution(mesh):
    placed = (
        P("groups", None),
        P(),
        P(None, "heads", None),
        P(None, "heads"),
        P(None, None, "heads"),
        P(None, "heads"),
    )
    return jax.shard_map(
        on_device, mesh=mesh, in_specs=placed, out_specs=P("groups", None), check_vma=False
    )
```

time: 957 us -> 323 us (0.34)
  waiting for transfers between devices: 555 us -> 221 us
  blocking collectives: 197 us -> 31.6 us
  local copies, waits for them, and re-layouts: 107 us -> 31.2 us
  starting transfers between devices: 50.9 us -> 0.09 us
    all_to_all x2 -> x0, waiting for transfers between devices: 494 us -> none  [the longest x1 433 us: on_device(): lax.all_to_all(w_in[0].reshape(shard_rows, 4, members, columns), 'heads',...]
    reduce_scatter x0 -> x1, waiting for transfers between devices: none -> 137 us  [on_device(): proj = lax.psum_scatter(partial, 'heads', scatter_dimension=0, tiled=False)]
    psum x1, blocking collectives: 132 us -> 31.6 us  [on_device(): total = lax.psum(jnp.sum(attn * attn, axis=1), 'heads')]
    unnamed x1 -> x0, blocking collectives: 65.5 us -> none
    unnamed x16 -> x10, local copies, waits for them, and re-layouts: 56 us -> 13.2 us
    all_to_all x2 -> x0, starting transfers between devices: 35.5 us -> none  [the longest x1 28.1 us: on_device(): lax.all_to_all(w_in[0].reshape(shard_rows, 4, members, columns), 'heads',...]
    all_to_all x2 -> x0, local copies, waits for them, and re-layouts: 30 us -> none  [the longest x1 21.3 us: on_device(): lax.all_to_all(w_in[0].reshape(shard_rows, 4, members, columns), 'heads',...]
    all_gather x1 -> x2, waiting for transfers between devices: 54.6 us -> 84.2 us  [the longest x1 42.5 us: on_device(): mixed_all = lax.all_gather(mixed, 'heads', axis=0, tiled=False)]
  transfers between devices with their start and end apart: 7 -> 3, of which waited for: 5 -> 3; matrix products, arithmetic and copies ran while one was open for 7% -> 0% of each run, Pallas kernels for 0% -> 0%
where the time goes in v1:
time: 323 us
  waiting for transfers between devices  221 us (68%)
  blocking collectives  31.6 us (10%)
  local copies, waits for them, and re-layouts  31.2 us (10%)
  matrix products  21.3 us (7%)
  between operations  13.2 us (4%)
  other arithmetic  4.49 us (1%)
    reduce_scatter x1, waiting for transfers between devices, on_device(): proj = lax.psum_scatter(partial, 'heads', scatter_dimension=0, tiled=False)  137 us
    all_gather x1, waiting for transfers between devices, on_device(): mixed_all = lax.all_gather(mixed, 'heads', axis=0, tiled=False)  42.5 us
    all_gather x1, waiting for transfers between devices, on_device(): return lax.all_gather(updated, 'heads', axis=1, tiled=True)  41.6 us
    psum x1, blocking collectives, on_device(): total = lax.psum(jnp.sum(attn * attn, axis=1), 'heads')  31.6 us
    reshape x1, local copies, waits for them, and re-layouts, on_device(): partial = partial.reshape(tokens, 4, members, columns).transpose(2, 0, 1, 3)  17 us
    dot_general x1, matrix products, on_device(): jnp.dot(normed, w_in[0], preferred_element_type=jnp.float32)  14.4 us
    unnamed x10, local copies, waits for them, and re-layouts  13.2 us
  transfers between devices with their start and end apart: 3, of which 3 were waited for; matrix products, arithmetic and copies ran while one was open for 0% of the time, Pallas kernels for 0%

profile of v1, /device:TPU:0, one launch (start us, length us, event | category | flops | bytes accessed | tf_op | source)
XLA Modules:
  0.0 322.9 jit_solution(6873202825005911337)
XLA Ops:
  6.5 0.0 copy-start
  6.5 0.0 reduce-scatter.2.cloned.1.call-start
  6.5 2.2 multiply_reduce_fusion
  8.8 0.0 copy-done
  8.8 14.4 %convolution_convert_fusion = bf16[192,32768]{1,0:T(8,128)(2,1)} fusion(bf16[1,384,32768]{2,1,0:T(8,128)(2,1)} %param.8, f32[384]{0:T(512)S(1)} %dynamic-slice_reduce_fusion, f32[192]{0:T(256)S(1)} %add_rsqrt_fusion.1, bf16[192,6144]{1,0:T(8,128)(2,1)} %param.6, s32[]{:T(128)S(6)} %select_n.9), kind=kOutput, calls=%fused_computation | convolution fusion | flops 4838424576 | bytes 37898500 | tf_op jit(solution)/shard_map/dot_general | solution.py:26
  23.2 9.4 %copy.30 = bf16[24,8,64,512]{3,2,1,0:T(8,128)(2,1)S(1)} copy(bf16[24,8,64,512]{3,1,2,0:T(8,128)(2,1)} %bitcast.38) | data formatting | bytes 25165824
  32.6 17.0 %copy.46 = bf16[192,4,16,512]{3,0,1,2:T(8,128)(2,1)} copy(bf16[192,4,16,512]{3,2,1,0:T(8,128)(2,1)S(1)} %bitcast.40) | data formatting | bytes 25165824 | tf_op jit(solution)/shard_map/reshape | solution.py:27
  49.6 0.0 copy-start.3
  49.6 0.0 reduce-scatter.2.cloned.1.call-update
  49.6 0.0 all-gather.3.cloned.1.call-start
  49.8 0.5 copy-done.3
  50.3 136.8 %reduce-scatter.2.cloned.1.call-done = bf16[1,192,4,512]{3,1,2,0:T(8,128)(2,1)} async-done(((bf16[16,192,4,512]{3,1,2,0:T(8,128)(2,1)}), bf16[1,192,4,512]{3,1,2,0:T(8,128)(2,1)}) %reduce-scatter.2.cloned.1.call-update) | async-done | bytes 786448 | tf_op jit(solution)/shard_map/reduce_scatter | solution.py:28
  187.1 1.3 bitcast_convert_fusion
  188.4 0.1 fusion.31
  188.5 0.1 squeeze.15
  188.7 0.1 squeeze.16
  188.8 0.0 copy-start.2
  188.8 0.1 squeeze.17
  189.0 0.7 multiply_reduce_fusion.1
  189.7 0.3 copy.29
  190.0 0.2 reshape.151
  190.2 31.6 %psum.7 = f32[192]{0:T(256)S(1)} all-reduce(f32[192]{0:T(256)S(1)} %get-tuple-element.8), channel_id=1, replica_groups=mesh['groups'=2,'heads'=16] {'heads'}, use_global_device_ids=true, to_apply=%region_3.4 | all-reduce | flops 192 | bytes 1536 | tf_op jit(solution)/shard_map/psum | solution.py:46
  221.8 0.0 copy-done.2
  221.8 0.8 fusion.17
  222.6 0.0 all-gather.3.cloned.1.call-update
  222.6 0.0 all-gather.5.cloned.1.call-start
  222.7 42.5 %all-gather.3.cloned.1.call-done = bf16[16,192,512]{2,1,0:T(8,128)(2,1)} async-done(((bf16[1,192,512]{2,1,0:T(8,128)(2,1)}), bf16[16,192,512]{2,1,0:T(8,128)(2,1)}) %all-gather.3.cloned.1.call-update) | async-done | bytes 3145744 | tf_op jit(solution)/shard_map/all_gather | solution.py:54
  265.2 0.0 copy-start.1
  265.2 6.2 %fusion.5 = bf16[192,384]{1,0:T(8,128)(2,1)} fusion(bf16[16,192,512]{2,1,0:T(8,128)(2,1)} %all-gather.3.cloned.1.call-done, bf16[16,512,384]{2,1,0:T(8,128)(2,1)} %bitcast.42, bf16[192,6144]{1,0:T(8,128)(2,1)} %param.6, s32[]{:T(128)S(6)} %select_n.9), kind=kOutput, calls=%fused_computation.10 | convolution fusion | flops 1208180736 | bytes 9732100 | tf_op jit(solution)/shard_map/mtc,mcd->td/dot_general | solution.py:56
  271.4 0.0 all-gather.5.cloned.1.call-update
  271.4 41.6 %all-gather.5.cloned.1.call-done = bf16[192,6144]{1,0:T(8,128)(2,1)} async-done(((bf16[192,384]{1,0:T(8,128)(2,1)}), bf16[192,6144]{1,0:T(8,128)(2,1)}) %all-gather.5.cloned.1.call-update) | async-done | bytes 2359312 | tf_op jit(solution)/shard_map/all_gather | solution.py:59
  313.0 3.3 %copy.48 = bf16[192,6144]{1,0:T(8,128)(2,1)} copy(bf16[192,6144]{1,0:T(8,128)(2,1)} %all-gather.5.cloned.1.call-done) | data formatting | bytes 4718592
  316.3 0.0 copy-done.1
  (6 shorter events, 0.1 us)
Async XLA Ops:
  6.5 2.2 copy-start
  6.5 180.6 %reduce-scatter.2.cloned.1.call-start = ((), (), s32[]{:S(2)}) async-start(), calls=%async_computation.1 | async-start | bytes 13369344 | tf_op jit(solution)/shard_map/reduce_scatter | solution.py:28
  49.6 0.7 copy-start.3
  49.6 215.6 %all-gather.3.cloned.1.call-start = ((), (), s32[]{:S(2)}) async-start(), calls=%async_computation.2 | async-start | bytes 3342336 | tf_op jit(solution)/shard_map/all_gather | solution.py:54
  188.8 32.9 %copy-start.2 = (f32[1,512]{1,0:T(1,128)S(1)}, f32[1,512]{1,0:T(1,128)}, u32[]{:S(2)}) copy-start(f32[1,512]{1,0:T(1,128)} %param.9) | copy-start | bytes 6148
  222.6 90.4 %all-gather.5.cloned.1.call-start = ((), (), s32[]{:S(2)}) async-start(), calls=%async_computation.3 | async-start | bytes 2506752 | tf_op jit(solution)/shard_map/all_gather | solution.py:59
  265.2 51.1 %copy-start.1 = (f32[1,6144]{1,0:T(1,128)S(1)}, f32[1,6144]{1,0:T(1,128)}, u32[]{:S(2)}) copy-start(f32[1,6144]{1,0:T(1,128)} %param.7) | copy-start | bytes 73732
Sparse Core Ops, SparseCore 0:
  49.7 137.2 reduce-scatter.1
  222.7 42.4 all-gather.2
  271.5 41.4 all-gather.4

commit v2 on v1

--- a/solution.py
+++ b/solution.py
@@ -1,9 +1,191 @@
+import functools
+
 import jax
 import jax.numpy as jnp
 from jax import lax
+from jax.experimental import pallas as pl
+from jax.experimental.pallas import tpu as pltpu
 from jax.sharding import PartitionSpec as P
 
-D = 6144
+KINDS = 4
+W_PARTS = 4
+
+
+def bit_orders(steps):
+    forward = tuple(range(steps))
+    turned = (0,) + tuple(range(2, steps)) + (1,)
+    return (forward, turned, forward, forward)
+
+
+def project_kernel(members, normed_ref, w_ref, out_ref, w_buf, part, got, w_sem, send_sem, recv_sem):
+    me = lax.axis_index("heads")
+    steps = members.bit_length() - 1
+    columns = out_ref.shape[2]
+    orders = bit_orders(steps)
+    width = members * columns
+
+    def my_bit(bit):
+        return lax.rem(me // (1 << bit), 2)
+
+    def partner(bit):
+        return me + (1 - 2 * my_bit(bit)) * (1 << bit)
+
+    def w_copy(kind, piece):
+        length = width // W_PARTS
+        return pltpu.make_async_copy(
+            w_ref.at[:, pl.ds(kind * width + piece * length, length)],
+            w_buf.at[kind % 2, :, pl.ds(piece * length, length)],
+            w_sem.at[kind, piece],
+        )
+
+    def w_start(kind):
+        for piece in range(W_PARTS):
+            w_copy(kind, piece).start()
+
+    w_start(0)
+    w_start(1)
+
+    barrier = pltpu.get_barrier_semaphore()
+    for bit in range(steps):
+        pl.semaphore_signal(barrier, inc=1, device_id={"heads": partner(bit)})
+    pl.semaphore_wait(barrier, steps)
+
+    def multiply(kind):
+        for piece in range(W_PARTS):
+            w_copy(kind, piece).wait()
+
+        @pl.loop(0, members)
+        def _(place):
+            owner = 0
+            for step, bit in enumerate(orders[kind]):
+                owner = owner + lax.rem(place // (1 << (steps - 1 - step)), 2) * (1 << bit)
+            begin = pl.multiple_of(owner * columns, columns)
+            block = jnp.dot(
+                normed_ref[...],
+                w_buf[kind % 2, :, pl.ds(begin, columns)],
+                preferred_element_type=jnp.float32,
+            )
+            part[kind, place] = block.astype(part.dtype)
+
+        if kind + 2 < KINDS:
+            w_start(kind + 2)
+
+    def layout(kind, step):
+        base = 0
+        for earlier in range(step):
+            base = base + my_bit(orders[kind][earlier]) * (members >> (earlier + 1))
+        length = members >> (step + 1)
+        bit = orders[kind][step]
+        keep = base + my_bit(bit) * length
+        give = base + (1 - my_bit(bit)) * length
+        return length, keep, give, members - (members >> step)
+
+    def remote(kind, step):
+        length, _, give, at = layout(kind, step)
+        return pltpu.make_async_remote_copy(
+            src_ref=part.at[kind, pl.ds(give, length)],
+            dst_ref=got.at[kind, pl.ds(at, length)],
+            send_sem=send_sem.at[kind, step],
+            recv_sem=recv_sem.at[kind, step],
+            device_id={"heads": partner(orders[kind][step])},
+        )
+
+    def send(kind, step):
+        remote(kind, step).start()
+
+    def arrive(kind, step):
+        remote(kind, step).wait_recv()
+
+    def add(kind, step):
+        length, keep, _, at = layout(kind, step)
+        if length == 1:
+            out_ref[kind] = part[kind, keep].astype(jnp.float32) + got[kind, at].astype(jnp.float32)
+            return
+
+        @pl.loop(0, length)
+        def _(index):
+            total = part[kind, keep + index].astype(jnp.float32) + got[kind, at + index].astype(
+                jnp.float32
+            )
+            part[kind, keep + index] = total.astype(part.dtype)
+
+    multiply(0)
+    send(0, 0)
+    multiply(1)
+    send(1, 0)
+    arrive(0, 0)
+    add(0, 0)
+    send(0, 1)
+    multiply(2)
+    send(2, 0)
+    arrive(1, 0)
+    add(1, 0)
+    send(1, 1)
+    multiply(3)
+    send(3, 0)
+    arrive(2, 0)
+    add(2, 0)
+    arrive(3, 0)
+    add(3, 0)
+    arrive(0, 1)
+    send(2, 1)
+    add(0, 1)
+    send(0, 2)
+    arrive(1, 1)
+    add(1, 1)
+    send(1, 2)
+    arrive(0, 2)
+    add(0, 2)
+    if steps > 3:
+        send(0, 3)
+    arrive(2, 1)
+    send(3, 1)
+    add(2, 1)
+    send(2, 2)
+    sent = {(0, s) for s in range(4)} | {(1, s) for s in range(3)} | {(2, s) for s in range(3)}
+    sent |= {(3, 0), (3, 1)}
+    taken = {(0, s) for s in range(3)} | {(1, 0), (1, 1), (2, 0), (2, 1), (3, 0)}
+    for step in range(1, steps):
+        for kind in (1, 2, 0, 3):
+            if (kind, step) in taken:
+                continue
+            arrive(kind, step)
+            add(kind, step)
+            if step + 1 < steps and (kind, step + 1) not in sent:
+                send(kind, step + 1)
+    for kind in range(KINDS):
+        for step in range(steps):
+            remote(kind, step).wait_send()
+
+
+def project(members, columns, normed, w_in):
+    tokens, rows = normed.shape
+    steps = members.bit_length() - 1
+    return pl.pallas_call(
+        functools.partial(project_kernel, members),
+        out_shape=jax.ShapeDtypeStruct((KINDS, tokens, columns), jnp.float32),
+        in_specs=[
+            pl.BlockSpec(memory_space=pltpu.VMEM),
+            pl.BlockSpec(memory_space=pl.ANY),
+        ],
+        out_specs=pl.BlockSpec(memory_space=pltpu.VMEM),
+        scratch_shapes=[
+            pltpu.VMEM((2, rows, members * columns), jnp.bfloat16),
+            pltpu.VMEM((KINDS, members, tokens, columns), jnp.bfloat16),
+            pltpu.VMEM((KINDS, members - 1, tokens, columns), jnp.bfloat16),
+            pltpu.SemaphoreType.DMA((KINDS, W_PARTS)),
+            pltpu.SemaphoreType.DMA((KINDS, steps)),
+            pltpu.SemaphoreType.DMA((KINDS, steps)),
+        ],
+        compiler_params=pltpu.CompilerParams(
+            collective_id=0, has_side_effects=True, vmem_limit_bytes=56 * 1024 * 1024
+        ),
+        cost_estimate=pl.CostEstimate(
+            flops=2 * tokens * rows * KINDS * members * columns,
+            bytes_accessed=2 * rows * KINDS * members * columns,
+            transcendentals=0,
+        ),
+    )(normed, w_in)
 
 
 def on_device(hidden, in_gain, w_in, attn_gain, w_out, slope_index):
@@ -23,15 +205,12 @@
     own_gain = lax.dynamic_slice_in_dim(in_gain, position * shard_rows, shard_rows, 1)
     normed = (own_hidden.astype(jnp.float32) * scale * own_gain).astype(jnp.bfloat16)
 
-    partial = jnp.dot(normed, w_in[0], preferred_element_type=jnp.float32).astype(jnp.bfloat16)
-    partial = partial.reshape(tokens, 4, members, columns).transpose(2, 0, 1, 3)
-    proj = lax.psum_scatter(partial, "heads", scatter_dimension=0, tiled=False)
-    proj = proj.astype(jnp.float32)
-
-    query = jax.nn.silu(proj[:, 0]).astype(jnp.bfloat16).reshape(tokens, heads_local, head_width)
-    keys = jax.nn.silu(proj[:, 1]).astype(jnp.bfloat16).reshape(tokens, heads_local, head_width)
-    values = jax.nn.silu(proj[:, 2]).astype(jnp.bfloat16).reshape(tokens, heads_local, head_width)
-    gate = proj[:, 3]
+    proj = project(members, columns, normed, w_in[0])
+
+    query = jax.nn.silu(proj[0]).astype(jnp.bfloat16).reshape(tokens, heads_local, head_width)
+    keys = jax.nn.silu(proj[1]).astype(jnp.bfloat16).reshape(tokens, heads_local, head_width)
+    values = jax.nn.silu(proj[2]).astype(jnp.bfloat16).reshape(tokens, heads_local, head_width)
+    gate = proj[3]
     slopes = jnp.exp2(-0.5 * slope_index[0].astype(jnp.float32))
     positions = jnp.arange(tokens, dtype=jnp.int32)
     offset = (positions[:, None] - positions[None, :]).astype(jnp.float32)

time: 323 us -> 241 us (0.75)
  waiting for transfers between devices: 221 us -> 84.3 us
  Pallas kernels: 0 us -> 94.1 us
  local copies, waits for them, and re-layouts: 31.2 us -> 5.48 us
  matrix products: 21.3 us -> 6.92 us
    reduce_scatter x1 -> x0, waiting for transfers between devices: 137 us -> none  [on_device(): proj = lax.psum_scatter(partial, 'heads', scatter_dimension=0, tiled=False)]
    pallas_call x0 -> x1, Pallas kernels: none -> 94.1 us  [project(): pl.pallas_call(functools.partial(project_kernel, members), out_shape=jax....]
    reshape x1 -> x0, local copies, waits for them, and re-layouts: 17 us -> none  [on_device(): partial = partial.reshape(tokens, 4, members, columns).transpose(2, 0, 1, 3)]
    dot_general x1 -> x0, matrix products: 14.4 us -> none  [on_device(): jnp.dot(normed, w_in[0], preferred_element_type=jnp.float32)]
    unnamed x10 -> x5, local copies, waits for them, and re-layouts: 13.2 us -> 3.31 us
  transfers between devices with their start and end apart: 3 -> 2, of which waited for: 3 -> 2; matrix products, arithmetic and copies ran while one was open for 0% -> 0% of each run, Pallas kernels for 0% -> 0%
where the time goes in v2:
time: 241 us; the launch traced here: 240 us
  Pallas kernels  94.1 us (39%)
  waiting for transfers between devices  84.3 us (35%)
  blocking collectives  29.5 us (12%)
  between operations  13.5 us (6%)
  matrix products  6.92 us (3%)
  other arithmetic  6.48 us (3%)
  local copies, waits for them, and re-layouts  5.48 us (2%)
    pallas_call x1, Pallas kernels, project(): pl.pallas_call(functools.partial(project_kernel, members), out_shape=jax....  94.1 us
    all_gather x1, waiting for transfers between devices, on_device(): mixed_all = lax.all_gather(mixed, 'heads', axis=0, tiled=False)  42.6 us
    all_gather x1, waiting for transfers between devices, on_device(): return lax.all_gather(updated, 'heads', axis=1, tiled=True)  41.6 us
    psum x1, blocking collectives, on_device(): total = lax.psum(jnp.sum(attn * attn, axis=1), 'heads')  29.5 us
    dot_general x1, matrix products, on_device(): jnp.einsum('mtc,mcd->td', mixed_all, w_blocks, preferred_element_type=jnp...  6.18 us
  transfers between devices with their start and end apart: 2, of which 2 were waited for; matrix products, arithmetic and copies ran while one was open for 0% of the time, Pallas kernels for 0%

profile of v2, /device:TPU:0, one launch (start us, length us, event | category | flops | bytes accessed | tf_op | source)
XLA Modules:
  0.0 240.3 jit_solution(6161543653773955827)
XLA Ops:
  6.5 0.0 copy-start
  6.5 0.0 all-gather.3.cloned.1.call-start
  6.6 0.7 negate_bitcast_fusion
  7.3 2.2 multiply_reduce_fusion
  9.5 0.0 copy-done
  9.6 1.7 fusion.13.normed_ref
  11.2 94.1 %shard_map.64 = f32[4,192,512]{2,1,0:T(8,128)} custom-call(bf16[192,384]{1,0:T(8,128)(2,1)} %fusion.13.normed_ref, bf16[384,32768]{1,0:T(8,128)(2,1)} %bitcast.15), custom_call_target="tpu_custom_call" | custom-call | flops 4831838208 | bytes 25165824 | tf_op jit(solution)/shard_map/pallas_call | solution.py:164
  105.4 1.3 fusion.19
  106.7 0.1 squeeze.17
  106.8 0.1 squeeze.16
  107.0 0.1 squeeze.15
  107.1 0.0 copy-start.1
  107.1 0.7 multiply_reduce_fusion.1
  107.9 29.5 %psum.7 = f32[192]{0:T(256)S(1)} all-reduce(f32[192]{0:T(256)S(1)} %get-tuple-element.8), channel_id=1, replica_groups=mesh['groups'=2,'heads'=16] {'heads'}, use_global_device_ids=true, to_apply=%region_2.3 | all-reduce | flops 192 | bytes 1536 | tf_op jit(solution)/shard_map/psum | solution.py:225
  137.4 0.3 copy.20
  137.6 0.2 reshape.114
  137.8 0.0 copy-done.1
  137.8 1.8 multiply_convert_fusion
  139.6 0.0 all-gather.3.cloned.1.call-update
  139.7 0.0 all-gather.5.cloned.1.call-start
  139.7 42.6 %all-gather.3.cloned.1.call-done = bf16[16,192,512]{2,1,0:T(8,128)(2,1)} async-done(((bf16[1,192,512]{2,1,0:T(8,128)(2,1)}), bf16[16,192,512]{2,1,0:T(8,128)(2,1)}) %all-gather.3.cloned.1.call-update) | async-done | bytes 3145744 | tf_op jit(solution)/shard_map/all_gather | solution.py:233
  182.3 6.2 %fusion.4 = bf16[192,384]{1,0:T(8,128)(2,1)} fusion(bf16[16,192,512]{2,1,0:T(8,128)(2,1)} %all-gather.3.cloned.1.call-done, bf16[16,512,384]{2,1,0:T(8,128)(2,1)} %bitcast.17, bf16[192,6144]{1,0:T(8,128)(2,1)} %param.6, s32[]{:T(128)S(6)} %select_n.9), kind=kOutput, calls=%fused_computation.7 | convolution fusion | flops 1208180736 | bytes 9732100 | tf_op jit(solution)/shard_map/mtc,mcd->td/dot_general | solution.py:235
  188.5 0.0 all-gather.5.cloned.1.call-update
  188.5 41.6 %all-gather.5.cloned.1.call-done = bf16[192,6144]{1,0:T(8,128)(2,1)} async-done(((bf16[192,384]{1,0:T(8,128)(2,1)}), bf16[192,6144]{1,0:T(8,128)(2,1)}) %all-gather.5.cloned.1.call-update) | async-done | bytes 2359312 | tf_op jit(solution)/shard_map/all_gather | solution.py:238
  230.2 3.3 %copy.36 = bf16[192,6144]{1,0:T(8,128)(2,1)} copy(bf16[192,6144]{1,0:T(8,128)(2,1)} %all-gather.5.cloned.1.call-done) | data formatting | bytes 4718592
  (5 shorter events, 0.1 us)
Async XLA Ops:
  6.5 3.0 %copy-start = (f32[1,6144]{1,0:T(1,128)S(1)}, f32[1,6144]{1,0:T(1,128)}, u32[]{:S(2)}) copy-start(f32[1,6144]{1,0:T(1,128)} %param.7) | copy-start | bytes 73732
  6.5 175.8 %all-gather.3.cloned.1.call-start = ((), (), s32[]{:S(2)}) async-start(), calls=%async_computation | async-start | bytes 3342336 | tf_op jit(solution)/shard_map/all_gather | solution.py:233
  107.1 30.7 %copy-start.1 = (f32[1,512]{1,0:T(1,128)S(1)}, f32[1,512]{1,0:T(1,128)}, u32[]{:S(2)}) copy-start(f32[1,512]{1,0:T(1,128)} %param.9) | copy-start | bytes 6148
  139.7 90.5 %all-gather.5.cloned.1.call-start = ((), (), s32[]{:S(2)}) async-start(), calls=%async_computation.1 | async-start | bytes 2506752 | tf_op jit(solution)/shard_map/all_gather | solution.py:238
Sparse Core Ops, SparseCore 0:
  139.8 42.4 all-gather.2
  188.6 41.4 all-gather.4

commit v3 on v2

--- a/solution.py
+++ b/solution.py
@@ -188,6 +188,187 @@
     )(normed, w_in)
 
 
+def output_kernel(
+    members, attn_width, scaled_ref, squares_ref, own_ref, w_ref, out_ref,
+    w_buf, mix, acc, res, tot, tot_got, w_sem, tot_sem, mix_send, mix_recv, res_send, res_recv,
+):
+    me = lax.axis_index("heads")
+    steps = members.bit_length() - 1
+    halves, _, tokens, half = mix.shape
+    columns = scaled_ref.shape[1]
+    res_rows = res.shape[2]
+    far_bits = tuple(range(steps - 1, 1, -1))
+    orders = (far_bits + (1, 0), (1,) + far_bits + (0,))
+
+    def my_bit(bit):
+        return lax.rem(me // (1 << bit), 2)
+
+    def partner(bit):
+        return me + (1 - 2 * my_bit(bit)) * (1 << bit)
+
+    w_rows = w_ref.shape[0] // W_PARTS
+
+    def w_copy(piece):
+        rows = pl.ds(piece * w_rows, w_rows)
+        return pltpu.make_async_copy(w_ref.at[rows], w_buf.at[rows], w_sem.at[piece])
+
+    for piece in range(W_PARTS):
+        w_copy(piece).start()
+
+    barrier = pltpu.get_barrier_semaphore()
+    for bit in range(steps):
+        pl.semaphore_signal(barrier, inc=1, device_id={"heads": partner(bit)})
+    pl.semaphore_wait(barrier, steps)
+
+    def total_copy(step):
+        return pltpu.make_async_remote_copy(
+            src_ref=tot.at[step],
+            dst_ref=tot_got.at[step],
+            send_sem=tot_sem.at[0, step],
+            recv_sem=tot_sem.at[1, step],
+            device_id={"heads": partner(step)},
+        )
+
+    tot[0] = squares_ref[...]
+    for step in range(steps):
+        total_copy(step).start()
+        total_copy(step).wait_recv()
+        tot[step + 1] = tot[step] + tot_got[step]
+    across = jnp.broadcast_to(tot[steps][:1], (tokens, tokens))
+    diagonal = lax.broadcasted_iota(jnp.int32, (tokens, tokens), 0) == lax.broadcasted_iota(
+        jnp.int32, (tokens, tokens), 1
+    )
+    total = jnp.sum(jnp.where(diagonal, across, 0.0), axis=1, keepdims=True)
+    norm = lax.rsqrt(total / attn_width + 1e-06)
+
+    def held(order, step):
+        base = 0
+        for later in range(step, steps):
+            base = base + my_bit(order[later]) * (1 << later)
+        return base
+
+    def incoming(order, step):
+        return held(order, step) + (1 - 2 * my_bit(order[step])) * (1 << step)
+
+    def owner_of(order, place):
+        owner = 0
+        for step, bit in enumerate(order):
+            owner = owner + lax.rem(place // (1 << step), 2) * (1 << bit)
+        return owner
+
+    def block_copy(buffer, sends, recvs, which, step, base):
+        run = pl.ds(base, 1 << step)
+        return pltpu.make_async_remote_copy(
+            src_ref=buffer.at[which, run],
+            dst_ref=buffer.at[which, run],
+            send_sem=sends.at[which, step],
+            recv_sem=recvs.at[which, step],
+            device_id={"heads": partner(orders[which][step])},
+        )
+
+    def mix_start(which, step):
+        block_copy(mix, mix_send, mix_recv, which, step, held(orders[which], step)).start()
+
+    def mix_arrive(which, step):
+        block_copy(mix, mix_send, mix_recv, which, step, incoming(orders[which], step)).wait_recv()
+
+    def res_start(which, step):
+        block_copy(res, res_send, res_recv, which, step, held(orders[which], step)).start()
+
+    def res_arrive(which, step):
+        block_copy(res, res_send, res_recv, which, step, incoming(orders[which], step)).wait_recv()
+
+    def multiply(which, first, count):
+        @pl.loop(0, count)
+        def _(index):
+            place = first + index
+            begin = pl.multiple_of(owner_of(orders[which], place) * columns + which * half, half)
+            acc[...] += jnp.dot(
+                mix[which, place], w_buf[pl.ds(begin, half)], preferred_element_type=jnp.float32
+            )
+
+    for which in range(halves):
+        lanes = slice(which * half, (which + 1) * half)
+        mix[which, held(orders[which], 0)] = (scaled_ref[:, lanes] * norm).astype(mix.dtype)
+        mix_start(which, 0)
+    acc[...] = own_ref[...].astype(jnp.float32)
+    for piece in range(W_PARTS):
+        w_copy(piece).wait()
+    for which in range(halves):
+        multiply(which, held(orders[which], 0), 1)
+    for step in range(steps):
+        for which in range(halves):
+            mix_arrive(which, step)
+            if step + 1 < steps:
+                mix_start(which, step + 1)
+            multiply(which, incoming(orders[which], step), 1 << step)
+
+    for which in range(2):
+        rows = slice(which * res_rows, (which + 1) * res_rows)
+        res[which, held(orders[which], 0)] = acc[rows].astype(res.dtype)
+        res_start(which, 0)
+
+    def put(which, first, count):
+        @pl.loop(0, count)
+        def _(index):
+            place = first + index
+            rows = slice(which * res_rows, (which + 1) * res_rows)
+            out_ref[owner_of(orders[which], place), rows] = res[which, place]
+
+    for which in range(2):
+        put(which, held(orders[which], 0), 1)
+    for step in range(steps):
+        for which in range(2):
+            res_arrive(which, step)
+            if step + 1 < steps:
+                res_start(which, step + 1)
+            put(which, incoming(orders[which], step), 1 << step)
+
+    for step in range(steps):
+        total_copy(step).wait_send()
+        for which in range(halves):
+            block_copy(mix, mix_send, mix_recv, which, step, held(orders[which], step)).wait_send()
+        for which in range(2):
+            block_copy(res, res_send, res_recv, which, step, held(orders[which], step)).wait_send()
+
+
+def output_rows(members, scaled, squares, own, w_out):
+    tokens, columns = scaled.shape
+    out_columns = own.shape[1]
+    steps = members.bit_length() - 1
+    halves = 2 if columns % 256 == 0 else 1
+    whole = pl.BlockSpec(memory_space=pltpu.VMEM)
+    blocks = pl.pallas_call(
+        functools.partial(output_kernel, members, columns * members),
+        out_shape=jax.ShapeDtypeStruct((members, tokens, out_columns), jnp.bfloat16),
+        in_specs=[whole, whole, whole, pl.BlockSpec(memory_space=pl.ANY)],
+        out_specs=whole,
+        scratch_shapes=[
+            pltpu.VMEM(w_out.shape, jnp.bfloat16),
+            pltpu.VMEM((halves, members, tokens, columns // halves), jnp.bfloat16),
+            pltpu.VMEM((tokens, out_columns), jnp.float32),
+            pltpu.VMEM((2, members, tokens // 2, out_columns), jnp.bfloat16),
+            pltpu.VMEM((steps + 1,) + squares.shape, jnp.float32),
+            pltpu.VMEM((steps,) + squares.shape, jnp.float32),
+            pltpu.SemaphoreType.DMA((W_PARTS,)),
+            pltpu.SemaphoreType.DMA((2, steps)),
+            pltpu.SemaphoreType.DMA((halves, steps)),
+            pltpu.SemaphoreType.DMA((halves, steps)),
+            pltpu.SemaphoreType.DMA((2, steps)),
+            pltpu.SemaphoreType.DMA((2, steps)),
+        ],
+        compiler_params=pltpu.CompilerParams(
+            collective_id=1, has_side_effects=True, vmem_limit_bytes=48 * 1024 * 1024
+        ),
+        cost_estimate=pl.CostEstimate(
+            flops=2 * tokens * w_out.shape[0] * out_columns,
+            bytes_accessed=2 * w_out.shape[0] * out_columns,
+            transcendentals=0,
+        ),
+    )(scaled, squares, own, w_out)
+    return blocks.transpose(1, 0, 2).reshape(tokens, members * out_columns)
+
+
 def on_device(hidden, in_gain, w_in, attn_gain, w_out, slope_index):
     members = lax.axis_size("heads")
     position = lax.axis_index("heads")
@@ -195,7 +376,6 @@
     columns = attn_gain.shape[1]
     heads_local = slope_index.shape[1]
     head_width = columns // heads_local
-    attn_width = columns * members
     out_columns = w_out.shape[2]
     widened = hidden.astype(jnp.float32)
     tokens = widened.shape[0]
@@ -222,20 +402,11 @@
     attn = jnp.einsum("hts,shd->thd", weights, values, preferred_element_type=jnp.float32).reshape(
         tokens, columns
     )
-    total = lax.psum(jnp.sum(attn * attn, axis=1), "heads")
-    mixed = (
-        attn
-        * lax.rsqrt(total[:, None] / attn_width + 1e-06)
-        * attn_gain[0][None, :]
-        * jax.nn.sigmoid(gate)
-    ).astype(jnp.bfloat16)
-
-    mixed_all = lax.all_gather(mixed, "heads", axis=0, tiled=False)
-    w_blocks = w_out[0].reshape(members, columns, out_columns)
-    update = jnp.einsum("mtc,mcd->td", mixed_all, w_blocks, preferred_element_type=jnp.float32)
+    squares = jnp.broadcast_to(jnp.sum(attn * attn, axis=1)[None, :], (8, tokens))
+    scaled = attn * attn_gain[0][None, :] * jax.nn.sigmoid(gate)
+
     own = lax.dynamic_slice_in_dim(hidden, position * out_columns, out_columns, 1)
-    updated = (own.astype(jnp.float32) + update).astype(jnp.bfloat16)
-    return lax.all_gather(updated, "heads", axis=1, tiled=True)
+    return output_rows(members, scaled, squares, own, w_out[0])
 
 
 def solution(mesh):

time: 241 us -> 164 us (0.68)
  waiting for transfers between devices: 84.3 us -> 0 us
  Pallas kernels: 94.1 us -> 153 us
  blocking collectives: 29.5 us -> 0 us
  between operations: 13.5 us -> 0.09 us
  matrix products: 6.92 us -> 0.74 us
    all_gather x2 -> x0, waiting for transfers between devices: 84.2 us -> none  [the longest x1 42.6 us: on_device(): mixed_all = lax.all_gather(mixed, 'heads', axis=0, tiled=False)]
    pallas_call x0 -> x1, Pallas kernels: none -> 58.9 us  [output_rows(): pl.pallas_call(functools.partial(output_kernel, members, columns * member...]
    psum x1 -> x0, blocking collectives: 29.5 us -> none  [on_device(): total = lax.psum(jnp.sum(attn * attn, axis=1), 'heads')]
    dot_general x1 -> x0, matrix products: 6.18 us -> none  [on_device(): jnp.einsum('mtc,mcd->td', mixed_all, w_blocks, preferred_element_type=jnp...]
    unnamed x5 -> x4, local copies, waits for them, and re-layouts: 3.31 us -> 0.01 us
  transfers between devices with their start and end apart: 2 -> 0, of which waited for: 2 -> 0; matrix products, arithmetic and copies ran while one was open for 0% -> 0% of each run, Pallas kernels for 0% -> 0%
where the time goes in v3:
time: 164 us; the launch traced here: 163 us
  Pallas kernels  153 us (93%)
  other arithmetic  5.77 us (4%)
  local copies, waits for them, and re-layouts  3.57 us (2%)
    pallas_call x1, Pallas kernels, project(): pl.pallas_call(functools.partial(project_kernel, members), out_shape=jax....  94.2 us
    pallas_call x1, Pallas kernels, output_rows(): pl.pallas_call(functools.partial(output_kernel, members, columns * member...  58.9 us

profile of v3, /device:TPU:0, one launch (start us, length us, event | category | flops | bytes accessed | tf_op | source)
XLA Modules:
  0.0 163.3 jit_solution(14703526847369312649)
XLA Ops:
  0.0 0.0 copy-start
  0.0 0.7 negate_bitcast_fusion
  0.7 2.2 %multiply_reduce_fusion = f32[192]{0:T(256)S(1)} fusion(bf16[192,6144]{1,0:T(8,128)(2,1)} %param.6), kind=kLoop, calls=%fused_computation | loop fusion | flops 3538752 | bytes 2360064 | tf_op jit(solution)/shard_map/reduce_sum | solution.py:383
  2.9 0.0 copy-done
  3.0 1.7 %multiply_convert_fusion.3 = (bf16[192,384]{1,0:T(8,128)(2,1)}, bf16[192,384]{1,0:T(8,128)(2,1)S(1)}) fusion(f32[384]{0:T(512)S(1)} %dynamic-slice_reduce_fusion, f32[192]{0:T(256)S(1)} %add_rsqrt_fusion, bf16[192,6144]{1,0:T(8,128)(2,1)} %param.6, s32[]{:T(128)S(6)} %select_n.9), kind=kLoop, calls=%fused_computation.18 | loop fusion | flops 294912 | bytes 444676 | tf_op jit(solution)/shard_map/convert_element_type | solution.py:386
  4.7 94.2 %shard_map.64 = f32[4,192,512]{2,1,0:T(8,128)} custom-call(bf16[192,384]{1,0:T(8,128)(2,1)} %get-tuple-element.5.normed_ref, bf16[384,32768]{1,0:T(8,128)(2,1)} %bitcast.22), custom_call_target="tpu_custom_call" | custom-call | flops 4831838208 | bytes 25165824 | tf_op jit(solution)/shard_map/pallas_call | solution.py:164
  98.9 1.3 fusion.16
  100.2 0.1 squeeze.20
  100.4 0.1 squeeze.19
  100.5 0.1 squeeze.18
  100.7 0.0 copy-start.1
  100.7 0.7 fusion.6
  101.4 0.0 copy-done.1
  101.4 1.1 fusion.5.scaled_ref
  102.6 58.9 %shard_map.65 = bf16[16,192,384]{2,1,0:T(8,128)(2,1)S(1)} custom-call(f32[192,512]{1,0:T(8,128)S(1)} %fusion.5.scaled_ref, f32[8,192]{1,0:T(8,128)S(1)} %broadcast_in_dim.16.squares_ref, bf16[192,384]{1,0:T(8,128)(2,1)S(1)} %get-tuple-element.6.own_ref, bf16[8192,384]{1,0:T(8,128)(2,1)} %bitcast.23), custom_call_target="tpu_custom_call" | custom-call | flops 1207959552 | bytes 6291456 | tf_op jit(solution)/shard_map/pallas_call | solution.py:341
  161.5 1.8 %copy.23 = bf16[16,24,8,384]{3,2,0,1:T(8,128)(2,1)} copy(bf16[16,24,8,384]{3,2,1,0:T(8,128)(2,1)S(1)} %bitcast.21) | data formatting | bytes 4718592 | tf_op jit(solution)/shard_map/reshape | solution.py:369
  (5 shorter events, 0.1 us)
Async XLA Ops:
  0.0 2.9 %copy-start = (f32[1,6144]{1,0:T(1,128)S(1)}, f32[1,6144]{1,0:T(1,128)}, u32[]{:S(2)}) copy-start(f32[1,6144]{1,0:T(1,128)} %param.7) | copy-start | bytes 73732
  100.7 0.8 copy-start.1

commit v4 on v3

--- a/solution.py
+++ b/solution.py
@@ -9,12 +9,60 @@
 
 KINDS = 4
 W_PARTS = 4
+HALVES = 2
 
 
 def bit_orders(steps):
     forward = tuple(range(steps))
     turned = (0,) + tuple(range(2, steps)) + (1,)
     return (forward, turned, forward, forward)
+
+
+def plan(steps):
+    orders = bit_orders(steps)
+    depth = {"core": 8, "y": 2, "z": 3}
+    free = dict.fromkeys(depth, 0.0)
+    flying = dict.fromkeys(depth, 0)
+    ready = {link: [] for link in depth}
+    landing = []
+    ops = []
+    now = 3.0
+    todo = list(range(KINDS))
+
+    def link_of(unit, step):
+        return ("core", "y")[orders[unit // HALVES][step]] if orders[unit // HALVES][step] < 2 else "z"
+
+    def launch(link):
+        while ready[link] and flying[link] < depth[link]:
+            unit, step = ready[link].pop(0)
+            bit = orders[unit // HALVES][step]
+            length = (1.6 if bit == 0 else 17.4 * max(1, bit - 1)) / (1 << step)
+            free[link] = max(free[link], now) + length
+            flying[link] += 1
+            landing.append((free[link] + 1.5, unit, step))
+            ops.append(("send", unit, step))
+
+    while todo or landing:
+        landing.sort()
+        if landing and (landing[0][0] <= now or not todo):
+            when, unit, step = landing.pop(0)
+            now = max(now, when)
+            link = link_of(unit, step)
+            flying[link] -= 1
+            ops.append(("arrive", unit, step))
+            launch(link)
+            ops.append(("add", unit, step))
+            now += 0.2 + 1.2 / (1 << step)
+            if step + 1 < steps:
+                ready[link_of(unit, step + 1)].append((unit, step + 1))
+                launch(link_of(unit, step + 1))
+        else:
+            kind = todo.pop(0)
+            ops.append(("multiply", kind))
+            now += 2.6
+            ready["core"] += [(kind * HALVES + half, 0) for half in range(HALVES)]
+            launch("core")
+    return ops
 
 
 def project_kernel(members, normed_ref, w_ref, out_ref, w_buf, part, got, w_sem, send_sem, recv_sem):
@@ -80,82 +128,50 @@
         give = base + (1 - my_bit(bit)) * length
         return length, keep, give, members - (members >> step)
 
-    def remote(kind, step):
+    half_rows = out_ref.shape[1] // HALVES
+
+    def rows_of(unit):
+        return pl.ds(unit % HALVES * half_rows, half_rows)
+
+    def remote(unit, step):
+        kind = unit // HALVES
         length, _, give, at = layout(kind, step)
         return pltpu.make_async_remote_copy(
-            src_ref=part.at[kind, pl.ds(give, length)],
-            dst_ref=got.at[kind, pl.ds(at, length)],
-            send_sem=send_sem.at[kind, step],
-            recv_sem=recv_sem.at[kind, step],
+            src_ref=part.at[kind, pl.ds(give, length), rows_of(unit)],
+            dst_ref=got.at[kind, pl.ds(at, length), rows_of(unit)],
+            send_sem=send_sem.at[unit, step],
+            recv_sem=recv_sem.at[unit, step],
             device_id={"heads": partner(orders[kind][step])},
         )
 
-    def send(kind, step):
-        remote(kind, step).start()
-
-    def arrive(kind, step):
-        remote(kind, step).wait_recv()
-
-    def add(kind, step):
+    def add(unit, step):
+        kind, rows = unit // HALVES, rows_of(unit)
         length, keep, _, at = layout(kind, step)
         if length == 1:
-            out_ref[kind] = part[kind, keep].astype(jnp.float32) + got[kind, at].astype(jnp.float32)
+            out_ref[kind, rows] = part[kind, keep, rows].astype(jnp.float32) + got[
+                kind, at, rows
+            ].astype(jnp.float32)
             return
 
         @pl.loop(0, length)
         def _(index):
-            total = part[kind, keep + index].astype(jnp.float32) + got[kind, at + index].astype(
-                jnp.float32
-            )
-            part[kind, keep + index] = total.astype(part.dtype)
-
-    multiply(0)
-    send(0, 0)
-    multiply(1)
-    send(1, 0)
-    arrive(0, 0)
-    add(0, 0)
-    send(0, 1)
-    multiply(2)
-    send(2, 0)
-    arrive(1, 0)
-    add(1, 0)
-    send(1, 1)
-    multiply(3)
-    send(3, 0)
-    arrive(2, 0)
-    add(2, 0)
-    arrive(3, 0)
-    add(3, 0)
-    arrive(0, 1)
-    send(2, 1)
-    add(0, 1)
-    send(0, 2)
-    arrive(1, 1)
-    add(1, 1)
-    send(1, 2)
-    arrive(0, 2)
-    add(0, 2)
-    if steps > 3:
-        send(0, 3)
-    arrive(2, 1)
-    send(3, 1)
-    add(2, 1)
-    send(2, 2)
-    sent = {(0, s) for s in range(4)} | {(1, s) for s in range(3)} | {(2, s) for s in range(3)}
-    sent |= {(3, 0), (3, 1)}
-    taken = {(0, s) for s in range(3)} | {(1, 0), (1, 1), (2, 0), (2, 1), (3, 0)}
-    for step in range(1, steps):
-        for kind in (1, 2, 0, 3):
-            if (kind, step) in taken:
-                continue
-            arrive(kind, step)
-            add(kind, step)
-            if step + 1 < steps and (kind, step + 1) not in sent:
-                send(kind, step + 1)
-    for kind in range(KINDS):
+            total = part[kind, keep + index, rows].astype(jnp.float32) + got[
+                kind, at + index, rows
+            ].astype(jnp.float32)
+            part[kind, keep + index, rows] = total.astype(part.dtype)
+
+    for name, *where in plan(steps):
+        if name == "multiply":
+            multiply(*where)
+        elif name == "send":
+            remote(*where).start()
+        elif name == "arrive":
+            remote(*where).wait_recv()
+        else:
+            add(*where)
+    for unit in range(KINDS * HALVES):
         for step in range(steps):
-            remote(kind, step).wait_send()
+            remote(unit, step).wait_send()
 
 
 def project(members, columns, normed, w_in):
@@ -174,8 +190,8 @@
             pltpu.VMEM((KINDS, members, tokens, columns), jnp.bfloat16),
             pltpu.VMEM((KINDS, members - 1, tokens, columns), jnp.bfloat16),
             pltpu.SemaphoreType.DMA((KINDS, W_PARTS)),
-            pltpu.SemaphoreType.DMA((KINDS, steps)),
-            pltpu.SemaphoreType.DMA((KINDS, steps)),
+            pltpu.SemaphoreType.DMA((KINDS * HALVES, steps)),
+            pltpu.SemaphoreType.DMA((KINDS * HALVES, steps)),
         ],
         compiler_params=pltpu.CompilerParams(
             collective_id=0, has_side_effects=True, vmem_limit_bytes=56 * 1024 * 1024

time: 164 us -> 169 us (1.030)
  Pallas kernels: 153 us -> 157 us
    pallas_call x1, Pallas kernels: 94.2 us -> 100 us  [project(): pl.pallas_call(functools.partial(project_kernel, members), out_shape=jax....]
    pallas_call x1, Pallas kernels: 58.9 us -> 56.7 us  [output_rows(): pl.pallas_call(functools.partial(output_kernel, members, columns * member...]
where the time goes in v4:
time: 169 us; the launch traced here: 167 us
  Pallas kernels  157 us (93%)
  other arithmetic  5.77 us (3%)
  local copies, waits for them, and re-layouts  3.57 us (2%)
    pallas_call x1, Pallas kernels, project(): pl.pallas_call(functools.partial(project_kernel, members), out_shape=jax....  100 us
    pallas_call x1, Pallas kernels, output_rows(): pl.pallas_call(functools.partial(output_kernel, members, columns * member...  56.7 us

profile of v4, /device:TPU:0, one launch (start us, length us, event | category | flops | bytes accessed | tf_op | source)
XLA Modules:
  0.0 167.0 jit_solution(15478330050967388868)
XLA Ops:
  0.0 0.0 copy-start
  0.0 0.7 negate_bitcast_fusion
  0.7 2.2 %multiply_reduce_fusion = f32[192]{0:T(256)S(1)} fusion(bf16[192,6144]{1,0:T(8,128)(2,1)} %param.6), kind=kLoop, calls=%fused_computation | loop fusion | flops 3538752 | bytes 2360064 | tf_op jit(solution)/shard_map/reduce_sum | solution.py:399
  2.9 0.0 copy-done
  3.0 1.7 %multiply_convert_fusion.3 = (bf16[192,384]{1,0:T(8,128)(2,1)}, bf16[192,384]{1,0:T(8,128)(2,1)S(1)}) fusion(f32[384]{0:T(512)S(1)} %dynamic-slice_reduce_fusion, f32[192]{0:T(256)S(1)} %add_rsqrt_fusion, bf16[192,6144]{1,0:T(8,128)(2,1)} %param.6, s32[]{:T(128)S(6)} %select_n.9), kind=kLoop, calls=%fused_computation.18 | loop fusion | flops 294912 | bytes 444676 | tf_op jit(solution)/shard_map/convert_element_type | solution.py:402
  4.7 100.1 %shard_map.64 = f32[4,192,512]{2,1,0:T(8,128)} custom-call(bf16[192,384]{1,0:T(8,128)(2,1)} %get-tuple-element.5.normed_ref, bf16[384,32768]{1,0:T(8,128)(2,1)} %bitcast.22), custom_call_target="tpu_custom_call" | custom-call | flops 4831838208 | bytes 25165824 | tf_op jit(solution)/shard_map/pallas_call | solution.py:180
  104.8 1.3 fusion.16
  106.1 0.1 squeeze.20
  106.2 0.1 squeeze.19
  106.4 0.1 squeeze.18
  106.5 0.0 copy-start.1
  106.5 0.7 fusion.6
  107.3 0.0 copy-done.1
  107.3 1.1 fusion.5.scaled_ref
  108.4 56.7 %shard_map.65 = bf16[16,192,384]{2,1,0:T(8,128)(2,1)S(1)} custom-call(f32[192,512]{1,0:T(8,128)S(1)} %fusion.5.scaled_ref, f32[8,192]{1,0:T(8,128)S(1)} %broadcast_in_dim.16.squares_ref, bf16[192,384]{1,0:T(8,128)(2,1)S(1)} %get-tuple-element.6.own_ref, bf16[8192,384]{1,0:T(8,128)(2,1)} %bitcast.23), custom_call_target="tpu_custom_call" | custom-call | flops 1207959552 | bytes 6291456 | tf_op jit(solution)/shard_map/pallas_call | solution.py:357
  165.2 1.8 %copy.23 = bf16[16,24,8,384]{3,2,0,1:T(8,128)(2,1)} copy(bf16[16,24,8,384]{3,2,1,0:T(8,128)(2,1)S(1)} %bitcast.21) | data formatting | bytes 4718592 | tf_op jit(solution)/shard_map/reshape | solution.py:385
  (5 shorter events, 0.1 us)
Async XLA Ops:
  0.0 2.9 %copy-start = (f32[1,6144]{1,0:T(1,128)S(1)}, f32[1,6144]{1,0:T(1,128)}, u32[]{:S(2)}) copy-start(f32[1,6144]{1,0:T(1,128)} %param.7) | copy-start | bytes 73732
  106.5 0.8 copy-start.1

commit v5 on v4

--- a/solution.py
+++ b/solution.py
@@ -10,17 +10,18 @@
 KINDS = 4
 W_PARTS = 4
 HALVES = 2
+TURNED = (1, 3)
 
 
 def bit_orders(steps):
     forward = tuple(range(steps))
     turned = (0,) + tuple(range(2, steps)) + (1,)
-    return (forward, turned, forward, forward)
+    return tuple(turned if unit in TURNED else forward for unit in range(KINDS * HALVES))
 
 
 def plan(steps):
     orders = bit_orders(steps)
-    depth = {"core": 8, "y": 2, "z": 3}
+    depth = {"core": 8, "y": 2, "near": 2, "far": 2}
     free = dict.fromkeys(depth, 0.0)
     flying = dict.fromkeys(depth, 0)
     ready = {link: [] for link in depth}
@@ -30,12 +31,12 @@
     todo = list(range(KINDS))
 
     def link_of(unit, step):
-        return ("core", "y")[orders[unit // HALVES][step]] if orders[unit // HALVES][step] < 2 else "z"
+        return ("core", "y", "near", "far")[min(orders[unit][step], 3)]
 
     def launch(link):
         while ready[link] and flying[link] < depth[link]:
             unit, step = ready[link].pop(0)
-            bit = orders[unit // HALVES][step]
+            bit = orders[unit][step]
             length = (1.6 if bit == 0 else 17.4 * max(1, bit - 1)) / (1 << step)
             free[link] = max(free[link], now) + length
             flying[link] += 1
@@ -52,14 +53,14 @@
             ops.append(("arrive", unit, step))
             launch(link)
             ops.append(("add", unit, step))
-            now += 0.2 + 1.2 / (1 << step)
+            now += 0.1 + 0.7 / (1 << step)
             if step + 1 < steps:
                 ready[link_of(unit, step + 1)].append((unit, step + 1))
                 launch(link_of(unit, step + 1))
         else:
             kind = todo.pop(0)
             ops.append(("multiply", kind))
-            now += 2.6
+            now += 5.5
             ready["core"] += [(kind * HALVES + half, 0) for half in range(HALVES)]
             launch("core")
     return ops
@@ -70,6 +71,7 @@
     steps = members.bit_length() - 1
     columns = out_ref.shape[2]
     orders = bit_orders(steps)
+    half_rows = out_ref.shape[1] // HALVES
     width = members * columns
 
     def my_bit(bit):
@@ -103,50 +105,50 @@
             w_copy(kind, piece).wait()
 
         @pl.loop(0, members)
-        def _(place):
-            owner = 0
-            for step, bit in enumerate(orders[kind]):
-                owner = owner + lax.rem(place // (1 << (steps - 1 - step)), 2) * (1 << bit)
+        def _(owner):
             begin = pl.multiple_of(owner * columns, columns)
             block = jnp.dot(
                 normed_ref[...],
                 w_buf[kind % 2, :, pl.ds(begin, columns)],
                 preferred_element_type=jnp.float32,
-            )
-            part[kind, place] = block.astype(part.dtype)
+            ).astype(part.dtype)
+            for half in range(HALVES):
+                place = 0
+                for step, bit in enumerate(orders[kind * HALVES + half]):
+                    place = place + lax.rem(owner // (1 << bit), 2) * (members >> (step + 1))
+                rows = slice(half * half_rows, (half + 1) * half_rows)
+                part[kind, place, rows] = block[rows]
 
         if kind + 2 < KINDS:
             w_start(kind + 2)
 
-    def layout(kind, step):
+    def layout(unit, step):
         base = 0
         for earlier in range(step):
-            base = base + my_bit(orders[kind][earlier]) * (members >> (earlier + 1))
+            base = base + my_bit(orders[unit][earlier]) * (members >> (earlier + 1))
         length = members >> (step + 1)
-        bit = orders[kind][step]
+        bit = orders[unit][step]
         keep = base + my_bit(bit) * length
         give = base + (1 - my_bit(bit)) * length
         return length, keep, give, members - (members >> step)
 
-    half_rows = out_ref.shape[1] // HALVES
-
     def rows_of(unit):
         return pl.ds(unit % HALVES * half_rows, half_rows)
 
     def remote(unit, step):
         kind = unit // HALVES
-        length, _, give, at = layout(kind, step)
+        length, _, give, at = layout(unit, step)
         return pltpu.make_async_remote_copy(
             src_ref=part.at[kind, pl.ds(give, length), rows_of(unit)],
             dst_ref=got.at[kind, pl.ds(at, length), rows_of(unit)],
             send_sem=send_sem.at[unit, step],
             recv_sem=recv_sem.at[unit, step],
-            device_id={"heads": partner(orders[kind][step])},
+            device_id={"heads": partner(orders[unit][step])},
         )
 
     def add(unit, step):
         kind, rows = unit // HALVES, rows_of(unit)
-        length, keep, _, at = layout(kind, step)
+        length, keep, _, at = layout(unit, step)
         if length == 1:
             out_ref[kind, rows] = part[kind, keep, rows].astype(jnp.float32) + got[
                 kind, at, rows

time: 169 us -> 157 us (0.929)
  Pallas kernels: 157 us -> 146 us
    pallas_call x1, Pallas kernels: 100 us -> 87.9 us  [project(): pl.pallas_call(functools.partial(project_kernel, members), out_shape=jax....]
where the time goes in v5:
time: 157 us; the launch traced here: 156 us
  Pallas kernels  146 us (93%)
  other arithmetic  5.77 us (4%)
  local copies, waits for them, and re-layouts  3.57 us (2%)
    pallas_call x1, Pallas kernels, project(): pl.pallas_call(functools.partial(project_kernel, members), out_shape=jax....  87.9 us
    pallas_call x1, Pallas kernels, output_rows(): pl.pallas_call(functools.partial(output_kernel, members, columns * member...  58.3 us

profile of v5, /device:TPU:0, one launch (start us, length us, event | category | flops | bytes accessed | tf_op | source)
XLA Modules:
  0.0 156.3 jit_solution(14079945770495424433)
XLA Ops:
  0.0 0.0 copy-start
  0.0 0.7 negate_bitcast_fusion
  0.7 2.2 %multiply_reduce_fusion = f32[192]{0:T(256)S(1)} fusion(bf16[192,6144]{1,0:T(8,128)(2,1)} %param.6), kind=kLoop, calls=%fused_computation | loop fusion | flops 3538752 | bytes 2360064 | tf_op jit(solution)/shard_map/reduce_sum | solution.py:401
  2.9 0.0 copy-done
  3.0 1.7 %multiply_convert_fusion.3 = (bf16[192,384]{1,0:T(8,128)(2,1)}, bf16[192,384]{1,0:T(8,128)(2,1)S(1)}) fusion(f32[384]{0:T(512)S(1)} %dynamic-slice_reduce_fusion, f32[192]{0:T(256)S(1)} %add_rsqrt_fusion, bf16[192,6144]{1,0:T(8,128)(2,1)} %param.6, s32[]{:T(128)S(6)} %select_n.9), kind=kLoop, calls=%fused_computation.18 | loop fusion | flops 294912 | bytes 444676 | tf_op jit(solution)/shard_map/convert_element_type | solution.py:404
  4.7 87.9 %shard_map.64 = f32[4,192,512]{2,1,0:T(8,128)} custom-call(bf16[192,384]{1,0:T(8,128)(2,1)} %get-tuple-element.5.normed_ref, bf16[384,32768]{1,0:T(8,128)(2,1)} %bitcast.22), custom_call_target="tpu_custom_call" | custom-call | flops 4831838208 | bytes 25165824 | tf_op jit(solution)/shard_map/pallas_call | solution.py:182
  92.6 1.3 fusion.16
  93.9 0.1 squeeze.20
  94.0 0.1 squeeze.19
  94.2 0.1 squeeze.18
  94.3 0.0 copy-start.1
  94.3 0.7 fusion.6
  95.1 0.0 copy-done.1
  95.1 1.1 fusion.5.scaled_ref
  96.2 58.3 %shard_map.65 = bf16[16,192,384]{2,1,0:T(8,128)(2,1)S(1)} custom-call(f32[192,512]{1,0:T(8,128)S(1)} %fusion.5.scaled_ref, f32[8,192]{1,0:T(8,128)S(1)} %broadcast_in_dim.16.squares_ref, bf16[192,384]{1,0:T(8,128)(2,1)S(1)} %get-tuple-element.6.own_ref, bf16[8192,384]{1,0:T(8,128)(2,1)} %bitcast.23), custom_call_target="tpu_custom_call" | custom-call | flops 1207959552 | bytes 6291456 | tf_op jit(solution)/shard_map/pallas_call | solution.py:359
  154.5 1.8 %copy.23 = bf16[16,24,8,384]{3,2,0,1:T(8,128)(2,1)} copy(bf16[16,24,8,384]{3,2,1,0:T(8,128)(2,1)S(1)} %bitcast.21) | data formatting | bytes 4718592 | tf_op jit(solution)/shard_map/reshape | solution.py:387
  (5 shorter events, 0.1 us)
Async XLA Ops:
  0.0 2.9 %copy-start = (f32[1,6144]{1,0:T(1,128)S(1)}, f32[1,6144]{1,0:T(1,128)}, u32[]{:S(2)}) copy-start(f32[1,6144]{1,0:T(1,128)} %param.7) | copy-start | bytes 73732
  94.3 0.8 copy-start.1

commit v6 on v5

--- a/solution.py
+++ b/solution.py
@@ -296,6 +296,55 @@
     def res_arrive(which, step):
         block_copy(res, res_send, res_recv, which, step, incoming(orders[which], step)).wait_recv()
 
+    def run_of(which, index):
+        if index == 0:
+            return held(orders[which], 0), 1
+        return incoming(orders[which], index - 1), 1 << (index - 1)
+
+    def sibling_run(which, index):
+        base, count = run_of(which, index)
+        return base + (1 - 2 * my_bit(0)) * (members // 2), count
+
+    def core_copy(buffer, sends, recvs, which, index, base, count):
+        run = pl.ds(base, count)
+        return pltpu.make_async_remote_copy(
+            src_ref=buffer.at[which, run],
+            dst_ref=buffer.at[which, run],
+            send_sem=sends.at[which, steps + index],
+            recv_sem=recvs.at[which, steps + index],
+            device_id={"heads": partner(0)},
+        )
+
+    def exchange(buffer, sends, recvs, pieces, start, arrive, use):
+        def share(which, index):
+            core_copy(buffer, sends, recvs, which, index, *run_of(which, index)).start()
+
+        def take(which, index):
+            base, count = sibling_run(which, index)
+            core_copy(buffer, sends, recvs, which, index, base, count).wait_recv()
+            use(which, base, count)
+
+        for which in range(pieces):
+            share(which, 0)
+            use(which, *run_of(which, 0))
+        for step in range(steps - 1):
+            for which in range(pieces):
+                arrive(which, step)
+                if step + 1 < steps - 1:
+                    start(which, step + 1)
+                share(which, step + 1)
+            for which in range(pieces):
+                use(which, *run_of(which, step + 1))
+                take(which, step)
+        for which in range(pieces):
+            take(which, steps - 1)
+        for which in range(pieces):
+            for step in range(steps - 1):
+                base = held(orders[which], step)
+                block_copy(buffer, sends, recvs, which, step, base).wait_send()
+            for index in range(steps):
+                core_copy(buffer, sends, recvs, which, index, *run_of(which, index)).wait_send()
+
     def multiply(which, first, count):
         @pl.loop(0, count)
         def _(index):
@@ -312,14 +361,7 @@
     acc[...] = own_ref[...].astype(jnp.float32)
     for piece in range(W_PARTS):
         w_copy(piece).wait()
-    for which in range(halves):
-        multiply(which, held(orders[which], 0), 1)
-    for step in range(steps):
-        for which in range(halves):
-            mix_arrive(which, step)
-            if step + 1 < steps:
-                mix_start(which, step + 1)
-            multiply(which, incoming(orders[which], step), 1 << step)
+    exchange(mix, mix_send, mix_recv, halves, mix_start, mix_arrive, multiply)
 
     for which in range(2):
         rows = slice(which * res_rows, (which + 1) * res_rows)
@@ -333,21 +375,9 @@
             rows = slice(which * res_rows, (which + 1) * res_rows)
             out_ref[owner_of(orders[which], place), rows] = res[which, place]
 
-    for which in range(2):
-        put(which, held(orders[which], 0), 1)
-    for step in range(steps):
-        for which in range(2):
-            res_arrive(which, step)
-            if step + 1 < steps:
-                res_start(which, step + 1)
-            put(which, incoming(orders[which], step), 1 << step)
-
+    exchange(res, res_send, res_recv, 2, res_start, res_arrive, put)
     for step in range(steps):
         total_copy(step).wait_send()
-        for which in range(halves):
-            block_copy(mix, mix_send, mix_recv, which, step, held(orders[which], step)).wait_send()
-        for which in range(2):
-            block_copy(res, res_send, res_recv, which, step, held(orders[which], step)).wait_send()
 
 
 def output_rows(members, scaled, squares, own, w_out):
@@ -370,10 +400,10 @@
             pltpu.VMEM((steps,) + squares.shape, jnp.float32),
             pltpu.SemaphoreType.DMA((W_PARTS,)),
             pltpu.SemaphoreType.DMA((2, steps)),
-            pltpu.SemaphoreType.DMA((halves, steps)),
-            pltpu.SemaphoreType.DMA((halves, steps)),
-            pltpu.SemaphoreType.DMA((2, steps)),
-            pltpu.SemaphoreType.DMA((2, steps)),
+            pltpu.SemaphoreType.DMA((halves, 2 * steps)),
+            pltpu.SemaphoreType.DMA((halves, 2 * steps)),
+            pltpu.SemaphoreType.DMA((2, 2 * steps)),
+            pltpu.SemaphoreType.DMA((2, 2 * steps)),
         ],
         compiler_params=pltpu.CompilerParams(
             collective_id=1, has_side_effects=True, vmem_limit_bytes=48 * 1024 * 1024

time: 157 us -> 154 us (0.981)
  Pallas kernels: 146 us -> 143 us
    pallas_call x1, Pallas kernels: 58.3 us -> 55.2 us  [output_rows(): pl.pallas_call(functools.partial(output_kernel, members, columns * member...]
where the time goes in v6:
time: 154 us; the launch traced here: 153 us
  Pallas kernels  143 us (93%)
  other arithmetic  5.77 us (4%)
  local copies, waits for them, and re-layouts  3.57 us (2%)
    pallas_call x1, Pallas kernels, project(): pl.pallas_call(functools.partial(project_kernel, members), out_shape=jax....  87.9 us
    pallas_call x1, Pallas kernels, output_rows(): pl.pallas_call(functools.partial(output_kernel, members, columns * member...  55.2 us

profile of v6, /device:TPU:0, one launch (start us, length us, event | category | flops | bytes accessed | tf_op | source)
XLA Modules:
  0.0 153.3 jit_solution(1340670903561381259)
XLA Ops:
  0.0 0.0 copy-start
  0.0 0.7 negate_bitcast_fusion
  0.7 2.2 %multiply_reduce_fusion = f32[192]{0:T(256)S(1)} fusion(bf16[192,6144]{1,0:T(8,128)(2,1)} %param.6), kind=kLoop, calls=%fused_computation | loop fusion | flops 3538752 | bytes 2360064 | tf_op jit(solution)/shard_map/reduce_sum | solution.py:431
  2.9 0.0 copy-done
  3.0 1.7 %multiply_convert_fusion.3 = (bf16[192,384]{1,0:T(8,128)(2,1)}, bf16[192,384]{1,0:T(8,128)(2,1)S(1)}) fusion(f32[384]{0:T(512)S(1)} %dynamic-slice_reduce_fusion, f32[192]{0:T(256)S(1)} %add_rsqrt_fusion, bf16[192,6144]{1,0:T(8,128)(2,1)} %param.6, s32[]{:T(128)S(6)} %select_n.9), kind=kLoop, calls=%fused_computation.18 | loop fusion | flops 294912 | bytes 444676 | tf_op jit(solution)/shard_map/convert_element_type | solution.py:434
  4.7 87.9 %shard_map.64 = f32[4,192,512]{2,1,0:T(8,128)} custom-call(bf16[192,384]{1,0:T(8,128)(2,1)} %get-tuple-element.5.normed_ref, bf16[384,32768]{1,0:T(8,128)(2,1)} %bitcast.22), custom_call_target="tpu_custom_call" | custom-call | flops 4831838208 | bytes 25165824 | tf_op jit(solution)/shard_map/pallas_call | solution.py:182
  92.6 1.3 fusion.16
  93.9 0.1 squeeze.20
  94.0 0.1 squeeze.19
  94.2 0.1 squeeze.18
  94.3 0.0 copy-start.1
  94.3 0.7 fusion.6
  95.1 0.0 copy-done.1
  95.1 1.1 fusion.5.scaled_ref
  96.2 55.2 %shard_map.65 = bf16[16,192,384]{2,1,0:T(8,128)(2,1)S(1)} custom-call(f32[192,512]{1,0:T(8,128)S(1)} %fusion.5.scaled_ref, f32[8,192]{1,0:T(8,128)S(1)} %broadcast_in_dim.16.squares_ref, bf16[192,384]{1,0:T(8,128)(2,1)S(1)} %get-tuple-element.6.own_ref, bf16[8192,384]{1,0:T(8,128)(2,1)} %bitcast.23), custom_call_target="tpu_custom_call" | custom-call | flops 1207959552 | bytes 6291456 | tf_op jit(solution)/shard_map/pallas_call | solution.py:389
  151.5 1.8 %copy.23 = bf16[16,24,8,384]{3,2,0,1:T(8,128)(2,1)} copy(bf16[16,24,8,384]{3,2,1,0:T(8,128)(2,1)S(1)} %bitcast.21) | data formatting | bytes 4718592 | tf_op jit(solution)/shard_map/reshape | solution.py:417
  (5 shorter events, 0.1 us)
Async XLA Ops:
  0.0 2.9 %copy-start = (f32[1,6144]{1,0:T(1,128)S(1)}, f32[1,6144]{1,0:T(1,128)}, u32[]{:S(2)}) copy-start(f32[1,6144]{1,0:T(1,128)} %param.7) | copy-start | bytes 73732
  94.3 0.8 copy-start.1
